TPU v7x, 128 devices: a whole 4x4x4 slice. The times are simulated.
128 devices in a mesh: head: 4 (over y), ctx: 32 (over x, z, core).
Axes of the slice: x: 4, y: 4, z: 4, core: 2. Of those that a mesh axis runs over, the one named last changes fastest.
Arguments:
- queries: bfloat16 [65536, 8192], P('ctx', 'head'), may hold values from -80 to 80
- keys_cache: bfloat16 [65536, 1024], P('ctx', 'head'), may hold values from -6 to 6
- values_cache: bfloat16 [65536, 1024], P('ctx', 'head'), may hold values from -6 to 6
- doc_ids: int32 [65536], replicated, may hold values from 0 to 3, as said below
- query_owner: int32 [2], replicated, may hold values from 0 to 31
- query_offset: int32 [2], replicated, may hold values from 0 to 1536
- out_weight: bfloat16 [8192, 8192], P('head', 'ctx'), may hold values from -0.25 to 0.25
Outputs:
- projected: bfloat16 [1024, 8192], P('head', 'ctx')
Inputs may be any that keep to these rules, and one draw needn't show every extreme that they name: `doc_ids`: document numbers never fall along the sequence and start at 0; the last document begins before position 1984.
All inputs are finite; a program needn't handle non-finite values.
Results may differ from a plain program's by a relative error of at most 0.0051.
Values may be sent and summed in bfloat16 or wider, within the bound.
A program may use at most 576 MiB of HBM per device.

v0:
```python
import math

import jax
import jax.numpy as jnp
from jax import lax
from jax.sharding import PartitionSpec as P

DH = 128
QC = 512
NCH = 2


def spread(array, axis, root):
    mine = lax.axis_index(axis) == root
    return lax.psum(jnp.where(mine, array, jnp.zeros_like(array)), axis)


def per_device(queries, keys_cache, values_cache, doc_ids, query_owner, query_offset, out_weight):
    my_rank = lax.axis_index("ctx")
    shard_len = keys_cache.shape[0]
    kv_heads = keys_cache.shape[1] // DH
    q_heads = queries.shape[1] // DH
    group_size = q_heads // kv_heads
    score_scale = 1.0 / math.sqrt(DH)
    key_heads = keys_cache.reshape(shard_len, kv_heads, DH)
    value_heads = values_cache.reshape(shard_len, kv_heads, DH)
    key_first = my_rank * shard_len
    key_pos = key_first + jnp.arange(shard_len, dtype=jnp.int32)
    key_doc = lax.dynamic_slice_in_dim(doc_ids, key_first, shard_len, 0)
    results = []
    for which in range(NCH):
        block_root = query_owner[which]
        own_rows = lax.dynamic_slice_in_dim(queries, query_offset[which], QC, 0)
        arrived = spread(own_rows, "ctx", block_root)
        start = block_root * shard_len + query_offset[which]
        query_pos = start + jnp.arange(QC, dtype=jnp.int32)
        query_doc = lax.dynamic_slice_in_dim(doc_ids, start, QC, 0)
        allowed = (key_pos[None, :] <= query_pos[:, None]) & (
            key_doc[None, :] == query_doc[:, None]
        )
        allowed = allowed[:, None, None, :]
        query_blocks = arrived.reshape(QC, kv_heads, group_size, DH)
        scores = (
            jnp.einsum(
                "qkgd,skd->qkgs", query_blocks, key_heads, preferred_element_type=jnp.float32
            )
            * score_scale
        )
        masked = jnp.where(allowed, scores, jnp.float32(-1e30))
        block_max = jnp.max(masked, axis=-1)
        weights = jnp.where(allowed, jnp.exp(masked - block_max[..., None]), jnp.float32(0.0))
        block_total = jnp.sum(weights, axis=-1).reshape(QC, q_heads)
        block_out = jnp.einsum(
            "qkgs,skd->qkgd",
            weights.astype(jnp.bfloat16),
            value_heads,
            preferred_element_type=jnp.float32,
        )
        block_out = block_out.reshape(QC, q_heads, DH)
        block_max = block_max.reshape(QC, q_heads)
        row_max = lax.pmax(block_max.astype(jnp.bfloat16), "ctx").astype(block_max.dtype)
        factor = jnp.exp(block_max - row_max)
        row_total, row_out = lax.psum((block_total * factor, block_out * factor[..., None]), "ctx")
        attention = (row_out / row_total[..., None]).reshape(QC, q_heads * DH).astype(jnp.bfloat16)
        results.append(attention)
    attention = jnp.concatenate(results, axis=0)
    summed = lax.psum_scatter(
        jnp.dot(attention, out_weight, preferred_element_type=jnp.float32),
        "head",
        scatter_dimension=0,
        tiled=True,
    )
    return summed.astype(jnp.bfloat16)


def solution(mesh):
    placed = (P("ctx", "head"), P("ctx", "head"), P("ctx", "head"), P(), P(), P(), P("head", "ctx"))
    return jax.shard_map(
        per_device, mesh=mesh, in_specs=placed, out_specs=P("head", "ctx"), check_vma=False
    )
```

profile of v0, /device:TPU:1, one launch (start us, length us, event | category | flops | bytes accessed | tf_op | source)
XLA Modules:
  0.0 690.4 jit_solution(18083013926466286358)
XLA Ops:
  6.5 1.4 fusion.39
  10.4 1.3 fusion.38
  13.0 4.8 constant_dynamic-slice_fusion.1
  17.8 3.9 copy.34
  22.3 1.5 broadcast_select_fusion.1
  23.8 3.9 copy.13
  27.7 2.5 copy.35
  30.9 2.4 copy.18
  36.1 2.1 reshape.145
  38.2 2.1 reshape.146
  40.3 0.7 dynamic_slice.15
  41.0 0.8 fusion.37
  41.8 1.8 compare_and_fusion.1
  43.7 105.7 %all-reduce.12.cloned.1.call-done = (bf16[512,2,8,128]{3,0,2,1:T(8,128)(2,1)}, bf16[512,2,8,128]{3,0,2,1:T(8,128)(2,1)}) async-done(((bf16[512,2,8,128]{3,0,2,1:T(8,128)(2,1)}, bf16[512,2,8,128]{3,0,2,1:T(8,128)(2,1)}), (bf16[512,2,8,128]{3,0,2,1:T(8,128)(2,1)}, bf16[512,2,8,128]{3,0,2,1:T(8,128)(2,1)})) %all-reduce.12.cloned.1.call-update) | async-done | bytes 4194320 | tf_op jit(solution)/shard_map/psum | solution.py:15
  149.4 25.4 %bitcast_reduce_fusion.1 = (f32[512,2,8]{0,2,1:T(8,128)S(1)}, f32[2,512,8,2048]{3,1,2,0:T(8,128)}) fusion(pred[512,2048]{1,0:T(8,128)(4,1)S(1)} %get-tuple-element.21, bf16[512,2,8,128]{3,0,2,1:T(8,128)(2,1)} %get-tuple-element.10, bf16[2048,2,128,1]{2,1,0,3:T(2,128)(2,1)} %bitcast.61), kind=kOutput, calls=%fused_computation.5 | convolution fusion | flops 4345290752 | bytes 71335936 | tf_op jit(solution)/shard_map/qkgd,skd->qkgs/dot_general | solution.py:44
  174.8 23.8 %bitcast_reduce_fusion = (f32[512,2,8]{0,2,1:T(8,128)S(1)}, f32[2,512,8,2048]{3,1,2,0:T(8,128)}) fusion(pred[512,2048]{1,0:T(8,128)(4,1)S(1)} %get-tuple-element.22, bf16[512,2,8,128]{3,0,2,1:T(8,128)(2,1)S(1)} %copy-done.4, bf16[2048,2,128,1]{2,1,0,3:T(2,128)(2,1)S(1)} %bitcast.62), kind=kOutput, calls=%fused_computation.1 | convolution fusion | flops 4345290752 | bytes 71335936 | tf_op jit(solution)/shard_map/qkgd,skd->qkgs/dot_general | solution.py:44
  198.6 42.6 %fusion.4 = (f32[512,2,8]{0,2,1:T(8,128)S(1)}, f32[512,2,8]{0,2,1:T(8,128)S(1)}) fusion(f32[2,512,8,2048]{3,1,2,0:T(8,128)} %get-tuple-element.30, f32[512,2,8]{0,2,1:T(8,128)S(1)} %get-tuple-element.29, pred[512,2048]{1,0:T(8,128)(4,1)S(1)} %get-tuple-element.21, f32[512,2,8]{0,2,1:T(8,128)S(1)} %get-tuple-element.27, ...), kind=kLoop, calls=%fused_computation.10 | loop fusion | flops 167755776 | bytes 136445952 | tf_op jit(solution)/shard_map/reduce_sum | solution.py:52
  241.2 30.8 %fusion.10 = f32[2,512,8,128]{3,1,2,0:T(8,128)} fusion(f32[2,512,8,2048]{3,1,2,0:T(8,128)} %get-tuple-element.30, f32[512,2,8]{0,2,1:T(8,128)S(1)} %get-tuple-element.29, pred[512,2048]{1,0:T(8,128)(4,1)S(1)} %get-tuple-element.21, bf16[2048,2,128,1]{2,1,0,3:T(2,128)(2,1)} %bitcast.69), kind=kOutput, calls=%fused_computation.15 | convolution fusion | flops 4378853376 | bytes 73433088 | tf_op jit(solution)/shard_map/qkgs,skd->qkgd/dot_general | solution.py:53
  272.0 25.9 %fusion.8 = f32[2,512,8,128]{3,1,2,0:T(8,128)} fusion(f32[2,512,8,2048]{3,1,2,0:T(8,128)} %get-tuple-element.28, f32[512,2,8]{0,2,1:T(8,128)S(1)} %get-tuple-element.27, pred[512,2048]{1,0:T(8,128)(4,1)S(1)} %get-tuple-element.22, bf16[2048,2,128,1]{2,1,0,3:T(2,128)(2,1)S(1)} %bitcast.70), kind=kOutput, calls=%fused_computation.14 | convolution fusion | flops 4378853376 | bytes 73433088 | tf_op jit(solution)/shard_map/qkgs,skd->qkgd/dot_general | solution.py:53
  297.9 5.4 copy.16
  303.3 5.4 copy.21
  308.7 122.3 %all-reduce.3 = (bf16[512,16]{0,1:T(8,128)(2,1)S(1)}, bf16[512,16]{0,1:T(8,128)(2,1)S(1)}) all-reduce(bf16[512,16]{0,1:T(8,128)(2,1)S(1)} %get-tuple-element.33, bf16[512,16]{0,1:T(8,128)(2,1)S(1)} %get-tuple-element.34), channel_id=1, replica_groups=mesh['head'=4,'ctx'=32] {'ctx'}, use_global_device_ids=true, to_apply=%region_8.9 | all-reduce | flops 16384 | bytes 65536 | tf_op jit(solution)/shard_map/pmax | solution.py:61
  431.6 0.6 bitcast_multiply_fusion
  432.3 4.9 broadcast_multiply_fusion.1
  437.2 2.8 broadcast_multiply_fusion
  440.4 89.3 %all-reduce.8.cloned.1.call-done = (f32[512,16]{0,1:T(8,128)}, f32[512,16]{0,1:T(8,128)}) async-done(((f32[512,16]{0,1:T(8,128)}, f32[512,16]{0,1:T(8,128)}), (f32[512,16]{0,1:T(8,128)}, f32[512,16]{0,1:T(8,128)})) %all-reduce.8.cloned.1.call-update) | async-done | bytes 65552 | tf_op jit(solution)/shard_map/psum | solution.py:63
  529.7 123.4 %all-reduce.10.cloned.1.call-done = (f32[512,16,128]{0,2,1:T(8,128)}, f32[512,16,128]{0,2,1:T(8,128)}) async-done(((f32[512,16,128]{0,2,1:T(8,128)}, f32[512,16,128]{0,2,1:T(8,128)}), (f32[512,16,128]{0,2,1:T(8,128)}, f32[512,16,128]{0,2,1:T(8,128)})) %all-reduce.10.cloned.1.call-update) | async-done | bytes 8388624 | tf_op jit(solution)/shard_map/psum | solution.py:63
  653.1 3.0 divide_convert_fusion.1
  656.5 1.4 divide_convert_fusion
  657.9 2.3 fusion.16
  660.2 22.0 %reduce-scatter.2.cloned.1.call-done = f32[256,256]{1,0:T(8,128)} async-done(((f32[1024,256]{1,0:T(8,128)}), f32[256,256]{1,0:T(8,128)}) %reduce-scatter.2.cloned.1.call-update) | async-done | bytes 262160 | tf_op jit(solution)/shard_map/reduce_scatter | solution.py:67
  682.2 1.6 convert_element_type.43
  (26 shorter events, 1.9 us)
Async XLA Ops:
  6.5 651.4 %copy-start = (bf16[2048,256]{1,0:T(8,128)(2,1)S(1)}, bf16[2048,256]{1,0:T(8,128)(2,1)}, u32[]{:S(2)}) copy-start(bf16[2048,256]{1,0:T(8,128)(2,1)} %param.13) | copy-start | bytes 3145732
  6.5 142.8 %all-reduce.12.cloned.1.call-start = ((), (), s32[]{:S(2)}) async-start(), calls=%async_computation.4 | async-start | bytes 8388608 | tf_op jit(solution)/shard_map/psum | solution.py:15
  33.4 496.3 %all-reduce.8.cloned.1.call-start = ((), (), s32[]{:S(2)}) async-start(), calls=%async_computation.2 | async-start | bytes 131072 | tf_op jit(solution)/shard_map/psum | solution.py:63
  149.4 25.4 %copy-start.2 = (bf16[2048,2,128]{2,1,0:T(2,128)(2,1)S(1)}, bf16[2048,2,128]{2,1,0:T(2,128)(2,1)}, u32[]{:S(2)}) copy-start(bf16[2048,2,128]{2,1,0:T(2,128)(2,1)} %reshape.145) | copy-start | bytes 3145732
  149.4 25.4 %copy-start.4 = (bf16[512,2,8,128]{3,0,2,1:T(8,128)(2,1)S(1)}, bf16[512,2,8,128]{3,0,2,1:T(8,128)(2,1)}, u32[]{:S(2)}) copy-start(bf16[512,2,8,128]{3,0,2,1:T(8,128)(2,1)} %get-tuple-element.9) | copy-start | bytes 6291460
  241.2 30.8 %copy-start.5 = (bf16[2048,2,128]{2,1,0:T(2,128)(2,1)S(1)}, bf16[2048,2,128]{2,1,0:T(2,128)(2,1)}, u32[]{:S(2)}) copy-start(bf16[2048,2,128]{2,1,0:T(2,128)(2,1)} %reshape.146) | copy-start | bytes 3145732
  432.3 220.8 %all-reduce.10.cloned.1.call-start = ((), (), s32[]{:S(2)}) async-start(), calls=%async_computation.3 | async-start | bytes 16777216 | tf_op jit(solution)/shard_map/psum | solution.py:63
  432.3 4.9 copy-start.1
  440.1 242.1 %reduce-scatter.2.cloned.1.call-start = ((), (), s32[]{:S(2)}) async-start(), calls=%async_computation.1 | async-start | bytes 1310720 | tf_op jit(solution)/shard_map/reduce_scatter | solution.py:67
  653.1 3.5 copy-start.3
Sparse Core Ops, SparseCore 0:
  33.5 115.8 all-reduce.11
  432.4 97.2 all-reduce.7
  533.6 119.4 all-reduce.9
  660.3 21.8 reduce-scatter.1
where the time goes:
time: 692 us; the launch traced here: 690 us
  waiting for transfers between devices  340 us (49%)
  blocking collectives  122 us (18%)
  matrix products  108 us (16%)
  other arithmetic  61 us (9%)
  local copies, waits for them, and re-layouts  37.2 us (5%)
  between operations  20.6 us (3%)
    psum x2, waiting for transfers between devices, per_device(): lax.psum((block_total * factor, block_out * factor[..., None]), 'ctx')  213 us
    pmax x1, blocking collectives, per_device(): lax.pmax(block_max.astype(jnp.bfloat16), 'ctx').astype(block_max.dtype)  122 us
    psum x1, waiting for transfers between devices, spread(): return lax.psum(jnp.where(mine, array, jnp.zeros_like(array)), axis)  106 us
    dot_general x2, matrix products, per_device(): jnp.einsum('qkgs,skd->qkgd', weights.astype(jnp.bfloat16), value_heads, p...  56.7 us
    dot_general x2, matrix products, per_device(): jnp.einsum('qkgd,skd->qkgs', query_blocks, key_heads, preferred_element_t...  49.2 us
    reduce_sum x1, other arithmetic, per_device(): block_total = jnp.sum(weights, axis=-1).reshape(QC, q_heads)  42.6 us
    reduce_scatter x1, waiting for transfers between devices, per_device(): lax.psum_scatter(jnp.dot(attention, out_weight, preferred_element_type=jn...  22 us
  transfers between devices with their start and end apart: 4, of which 4 were waited for; matrix products, arithmetic and copies ran while one was open for 2% of the time, Pallas kernels for 0%

commit v1 on v0

v1 whole, which is shorter than its diff:
```python
import functools
import math

import jax
import jax.numpy as jnp
from jax import lax
from jax.experimental import pallas as pl
from jax.experimental.pallas import tpu as pltpu
from jax.sharding import PartitionSpec as P

DH = 128
QC = 512
NCH = 2
R = 128
NC = NCH * QC // R
G = 8
MT = 512
HIDE = -1e30
SCALE = math.log2(math.e) / math.sqrt(DH)
MESH = pl.DeviceIdType.MESH
LEAD = 6
TRAIL = 6

S0, S1, S2, G1, G2, G3, O0, O1, O2, H1, H2, H3, Y = range(13)


def kernel(
    q_own, k_ref, v_ref, w_ref, lo_ref, hi_ref, out_ref,
    kx, vx, qx, s_buf, p_buf,
    u_buf, r1, t_buf, r2, q_full,
    o_send, o_recv, o_own, o_mix, o_two, w_col, o1_send, r1o, o2_send, r2o, a_full,
    y_send, y_recv, send, recv,
):
    shard = k_ref.shape[0]
    me = lax.axis_index("ctx")
    hd = lax.axis_index("head")
    core = lax.rem(me, 2)
    z = lax.rem(me // 2, 4)
    x = me // 8
    mine, theirs = core * G, (1 - core) * G

    def at_x(d):
        return {"ctx": (lax.rem(x + d, 4) * 4 + z) * 2 + core}

    def at_z(d):
        return {"ctx": (x * 4 + lax.rem(z + d, 4)) * 2 + core}

    partner = {"ctx": me + 1 - 2 * core}

    def at_y(d):
        return {"head": lax.rem(hd + d, 4)}

    barrier = pltpu.get_barrier_semaphore()
    for d in (1, 2, 3):
        for dev in (at_x(d), at_z(d), at_y(d)):
            pl.semaphore_signal(barrier, inc=1, device_id=dev, device_id_type=MESH)
    pl.semaphore_signal(barrier, inc=1, device_id=partner, device_id_type=MESH)

    eye = lax.broadcasted_iota(jnp.int32, (R, R), 0) == lax.broadcasted_iota(jnp.int32, (R, R), 1)
    for j in range(2):
        kx[j, 0:DH, :] = k_ref[:, j * DH : (j + 1) * DH].T
        vx[j, :, 0:DH] = v_ref[:, j * DH : (j + 1) * DH]
        vx[j, :, DH : 2 * DH] = jnp.ones((shard, DH), jnp.bfloat16)
    for g in range(G):
        qx[g * R : (g + 1) * R, DH : 2 * DH] = jnp.where(eye, 1.0, 0.0).astype(jnp.bfloat16)

    pl.semaphore_wait(barrier, 10)

    def put(src, dst, step, c, dev):
        pltpu.make_async_remote_copy(
            src_ref=src, dst_ref=dst, send_sem=send.at[step, c], recv_sem=recv.at[step, c],
            device_id=dev, device_id_type=MESH,
        ).start()

    def get(like, step, c):
        pltpu.make_async_copy(like, like, send.at[step, c]).wait()
        pltpu.make_async_copy(like, like, recv.at[step, c]).wait()

    def rows(c):
        return pl.ds(pl.multiple_of(c * R, R), R)

    def quarter(i):
        return pl.ds(pl.multiple_of(i * 32, 32), 32)

    def q0_start(c):
        put(q_own.at[pl.ds(theirs, G), rows(c)], u_buf.at[c], S0, c, partner)

    def q1_start(c):
        get(u_buf.at[c], S0, c)
        for g in range(G):
            u_buf[c, g] = u_buf[c, g] + q_own[mine + g, rows(c), :]
        for d in (1, 2, 3):
            put(u_buf.at[c, lax.rem(x + d, 4)], r1.at[c, d - 1], S1, c, at_x(d))
            put(u_buf.at[c, 4 + lax.rem(z + d, 4)], r1.at[c, 2 + d], S1, c, at_z(d))

    def q2_start(c):
        get(r1.at[c], S1, c)
        t_buf[c, 0] = (u_buf[c, x] + r1[c, 0]) + (r1[c, 1] + r1[c, 2])
        t_buf[c, 1] = (u_buf[c, 4 + z] + r1[c, 3]) + (r1[c, 4] + r1[c, 5])
        for d in (1, 2, 3):
            put(t_buf.at[c, 0, quarter(lax.rem(z + d, 4))], r2.at[c, d - 1], S2, c, at_z(d))
            put(t_buf.at[c, 1, quarter(lax.rem(x + d, 4))], r2.at[c, 2 + d], S2, c, at_x(d))

    def gather1(full, c, step):
        a = full.at[c, mine + x, quarter(z)]
        b = full.at[c, mine + 4 + z, quarter(x)]
        for d in (1, 2, 3):
            put(a, a, step, c, at_z(d))
            put(b, b, step, c, at_x(d))

    def gather2(full, c, step):
        get(r2.at[c], step - 1, c)
        a, b = full.at[c, mine + x], full.at[c, mine + 4 + z]
        for d in (1, 2, 3):
            put(a, a, step, c, at_x(d))
            put(b, b, step, c, at_z(d))

    def gather3(full, c, step):
        get(r1.at[c], step - 1, c)
        half = full.at[c, pl.ds(mine, G)]
        put(half, half, step, c, partner)

    def q3_start(c):
        get(r2.at[c], S2, c)
        q_full[c, mine + x, quarter(z), :] = (t_buf[c, 0, quarter(z), :] + r2[c, 0]) + (r2[c, 1] + r2[c, 2])
        q_full[c, mine + 4 + z, quarter(x), :] = (t_buf[c, 1, quarter(x), :] + r2[c, 3]) + (r2[c, 4] + r2[c, 5])
        gather1(q_full, c, G1)

    def hide(c):
        lo = jnp.broadcast_to(lo_ref[pl.ds(c, 1), :], (R, R)).T
        hi = jnp.broadcast_to(hi_ref[pl.ds(c, 1), :], (R, R)).T
        lane = lax.broadcasted_iota(jnp.int32, (R, R), 1).astype(jnp.float32)
        for i in range(shard // R):
            pos = lane + float(i * R)
            bias = jnp.where((pos >= lo) & (pos <= hi), 0.0, HIDE).astype(jnp.bfloat16)
            for j in range(2):
                kx[j, DH : 2 * DH, i * R : (i + 1) * R] = bias

    def attend(c, j, dest):
        first = j * G
        for g in range(G):
            qx[g * R : (g + 1) * R, 0:DH] = q_full[c, first + g]
        tiles = G * R // MT

        def score(t):
            s_buf[t] = jnp.dot(qx[t * MT : (t + 1) * MT, :], kx[j], preferred_element_type=jnp.float32)

        score(0)
        for t in range(tiles):
            if t + 1 < tiles:
                score(t + 1)
            s = s_buf[t]
            top = jnp.max(s, axis=1, keepdims=True) * SCALE
            p_buf[t] = jnp.exp2(s * SCALE - top).astype(jnp.bfloat16)
            o = jnp.dot(p_buf[t], vx[j], preferred_element_type=jnp.float32)
            total = o[:, DH : 2 * DH]
            mean = o[:, 0:DH] / total
            lse = top + jnp.log2(total)
            for i in range(MT // R):
                g = t * (MT // R) + i
                dest[g, 0:R, :] = mean[i * R : (i + 1) * R]
                flat = jnp.sum(jnp.where(eye, lse[i * R : (i + 1) * R], 0.0), axis=0, keepdims=True)
                dest[g, R : R + 8, :] = jnp.broadcast_to(flat, (8, R))

    def column(v):
        return jnp.broadcast_to(v, (R, R)).T

    def merge_stats(parts):
        top = functools.reduce(jnp.maximum, parts)
        ws = [jnp.exp2(p - top) for p in parts]
        total = functools.reduce(jnp.add, ws)
        return [w / total for w in ws], top + jnp.log2(total)

    def pieces3(v):
        a = v.astype(jnp.bfloat16)
        rest = v - a.astype(jnp.float32)
        b = rest.astype(jnp.bfloat16)
        c = (rest - b.astype(jnp.float32)).astype(jnp.bfloat16)
        row = lax.broadcasted_iota(jnp.int32, (16, R), 0)
        full = [jnp.broadcast_to(p.astype(jnp.float32), (16, R)) for p in (a, b, c)]
        return jnp.where(row == 0, full[0], jnp.where(row == 1, full[1], jnp.where(row == 2, full[2], 0.0))).astype(jnp.bfloat16)

    def whole3(block):
        f = block.astype(jnp.float32)
        return (f[0:1] + f[1:2]) + f[2:3]

    def o1_start(c):
        get(o_recv.at[c], O0, c)
        for g in range(G):
            (wa, wb), lse = merge_stats([o_own[g, R : R + 1, :], o_recv[c, g, R : R + 1, :]])
            mixed = o_own[g, 0:R, :] * column(wa) + o_recv[c, g, 0:R, :] * column(wb)
            o_mix[g, 0:R, :] = mixed
            o_mix[g, R : R + 8, :] = jnp.broadcast_to(lse, (8, R))
            o1_send[c, g, 0:R, :] = mixed.astype(jnp.bfloat16)
            o1_send[c, g, R : R + 16, :] = pieces3(lse)
        for d in (1, 2, 3):
            put(o1_send.at[c, lax.rem(x + d, 4)], r1o.at[c, d - 1], O1, c, at_x(d))
            put(o1_send.at[c, 4 + lax.rem(z + d, 4)], r1o.at[c, 2 + d], O1, c, at_z(d))

    def o2_start(c):
        get(r1o.at[c], O1, c)
        for i, at in ((0, x), (1, 4 + z)):
            stats = [o_mix[at, R : R + 1, :]] + [whole3(r1o[c, 3 * i + d, R : R + 16, :]) for d in range(3)]
            ws, lse = merge_stats(stats)
            mixed = o_mix[at, 0:R, :] * column(ws[0])
            for d in range(3):
                mixed += r1o[c, 3 * i + d, 0:R, :].astype(jnp.float32) * column(ws[1 + d])
            o_two[i, 0:R, :] = mixed
            o_two[i, R : R + 8, :] = jnp.broadcast_to(lse, (8, R))
            coded = pieces3(lse)
            for q in range(4):
                o2_send[c, i, q, 0:32, :] = mixed[q * 32 : (q + 1) * 32].astype(jnp.bfloat16)
                o2_send[c, i, q, 32:48, :] = coded
        for d in (1, 2, 3):
            zd, xd = lax.rem(z + d, 4), lax.rem(x + d, 4)
            put(o2_send.at[c, 0, zd], r2o.at[c, d - 1], O2, c, at_z(d))
            put(o2_send.at[c, 1, xd], r2o.at[c, 2 + d], O2, c, at_x(d))

    def o3_start(c):
        get(r2o.at[c], O2, c)
        for i, at, part in ((0, x, z), (1, 4 + z, x)):
            stats = [o_two[i, R : R + 1, :]] + [whole3(r2o[c, 3 * i + d, 32:48, :]) for d in range(3)]
            ws, _ = merge_stats(stats)
            for d in range(4):
                w_col[d] = column(ws[d])
            mixed = o_two[i, quarter(part), :] * w_col[0, quarter(part), :]
            for d in range(3):
                mixed += r2o[c, 3 * i + d, 0:32, :].astype(jnp.float32) * w_col[1 + d, quarter(part), :]
            a_full[c, mine + at, quarter(part), :] = mixed.astype(jnp.bfloat16)
        gather1(a_full, c, H1)

    def project(c):
        get(a_full.at[c, pl.ds(0, G)], H3, c)
        acc = jnp.zeros((R, w_ref.shape[1]), jnp.float32)
        for h in range(2 * G):
            acc += jnp.dot(a_full[c, h], w_ref[h * DH : (h + 1) * DH, :], preferred_element_type=jnp.float32)
        y_send[c] = acc
        owner = c // 2
        slot = lax.rem(c, 2)
        d = lax.rem(owner - hd + 4, 4)

        @pl.when(d > 0)
        def _():
            put(y_send.at[c], y_recv.at[d - 1, slot], Y, c, at_y(d))

    def slot(t, carry):
        def when(c, do):
            pl.when((c >= 0) & (c < NC))(functools.partial(do, c))

        when(t, lambda c: get(u_buf.at[c], G3, c))
        when(t + 1, lambda c: gather3(q_full, c, G3))
        when(t + 2, lambda c: gather2(q_full, c, G2))
        when(t + 3, q3_start)
        when(t + 4, q2_start)
        when(t + 5, q1_start)
        when(t + 6, q0_start)

        def first(c):
            hide(c)
            attend(c, 1 - core, o_send)
            put(o_send, o_recv.at[c], O0, c, partner)

        when(t, first)
        when(t, lambda c: attend(c, core, o_own))
        when(t - 5, project)
        when(t - 4, lambda c: gather3(a_full, c, H3))
        when(t - 3, lambda c: gather2(a_full, c, H2))
        when(t - 2, o3_start)
        when(t - 1, o2_start)
        when(t, o1_start)
        return carry

    lax.fori_loop(-LEAD, NC + TRAIL - 1, slot, 0)

    for c in range(NC):
        d = lax.rem(c // 2 - hd + 4, 4)

        @pl.when(d > 0)
        def _():
            pltpu.make_async_copy(y_send.at[c], y_send.at[c], send.at[Y, c]).wait()

    for i in range(2):
        c = hd * 2 + i
        pltpu.make_async_copy(y_recv.at[:, i], y_recv.at[:, i], recv.at[Y, c]).wait()
        total = (y_send[c] + y_recv[0, i]) + (y_recv[1, i] + y_recv[2, i])
        out_ref[i * R : (i + 1) * R, :] = total.astype(jnp.bfloat16)


def per_device(queries, keys_cache, values_cache, doc_ids, query_owner, query_offset, out_weight):
    me = lax.axis_index("ctx")
    shard = keys_cache.shape[0]
    starts = query_owner * shard + query_offset
    own, positions, docs = [], [], []
    for which in range(NCH):
        block = lax.dynamic_slice_in_dim(queries, query_offset[which], QC, 0)
        own.append(jnp.where(query_owner[which] == me, block, jnp.zeros_like(block)))
        positions.append(starts[which] + jnp.arange(QC, dtype=jnp.int32))
        docs.append(lax.dynamic_slice_in_dim(doc_ids, starts[which], QC, 0))
    q_own = jnp.concatenate(own, 0).reshape(NC * R, 2 * G, DH).transpose(1, 0, 2)
    position, doc = jnp.concatenate(positions), jnp.concatenate(docs)
    early = doc_ids[:shard]
    begin = jnp.zeros_like(position)
    for d in range(1, 4):
        begin = jnp.where(doc == d, jnp.sum((early < d).astype(jnp.int32)), begin)
    lo = (begin - me * shard).astype(jnp.float32).reshape(NC, R)
    hi = (position - me * shard).astype(jnp.float32).reshape(NC, R)

    width = out_weight.shape[1]
    bf, f32 = jnp.bfloat16, jnp.float32
    scratch = [
        pltpu.VMEM((2, 2 * DH, shard), bf),
        pltpu.VMEM((2, shard, 2 * DH), bf),
        pltpu.VMEM((G * R, 2 * DH), bf),
        pltpu.VMEM((2, MT, shard), f32),
        pltpu.VMEM((2, MT, shard), bf),
        pltpu.VMEM((NC, G, R, DH), bf),
        pltpu.VMEM((NC, 6, R, DH), bf),
        pltpu.VMEM((NC, 2, R, DH), bf),
        pltpu.VMEM((NC, 6, 32, DH), bf),
        pltpu.VMEM((NC, 2 * G, R, DH), bf),
        pltpu.VMEM((G, R + 8, DH), f32),
        pltpu.VMEM((NC, G, R + 8, DH), f32),
        pltpu.VMEM((G, R + 8, DH), f32),
        pltpu.VMEM((G, R + 8, DH), f32),
        pltpu.VMEM((2, R + 8, DH), f32),
        pltpu.VMEM((4, R, DH), f32),
        pltpu.VMEM((NC, G, R + 16, DH), bf),
        pltpu.VMEM((NC, 6, R + 16, DH), bf),
        pltpu.VMEM((NC, 2, 4, 48, DH), bf),
        pltpu.VMEM((NC, 6, 48, DH), bf),
        pltpu.VMEM((NC, 2 * G, R, DH), bf),
        pltpu.VMEM((NC, R, width), f32),
        pltpu.VMEM((3, 2, R, width), f32),
        pltpu.SemaphoreType.DMA((13, NC)),
        pltpu.SemaphoreType.DMA((13, NC)),
    ]
    vmem = pl.BlockSpec(memory_space=pltpu.VMEM)
    return pl.pallas_call(
        kernel,
        out_shape=jax.ShapeDtypeStruct((NC * R // 4, width), bf),
        in_specs=[vmem] * 6,
        out_specs=vmem,
        scratch_shapes=scratch,
        compiler_params=pltpu.CompilerParams(
            collective_id=0, has_side_effects=True, vmem_limit_bytes=60 * 2**20
        ),
    )(q_own, keys_cache, values_cache, out_weight, lo, hi)


def solution(mesh):
    placed = (P("ctx", "head"), P("ctx", "head"), P("ctx", "head"), P(), P(), P(), P("head", "ctx"))
    return jax.shard_map(
        per_device, mesh=mesh, in_specs=placed, out_specs=P("head", "ctx"), check_vma=False
    )
```

time: 692 us -> 159 us (0.23)
  waiting for transfers between devices: 340 us -> 0 us
  blocking collectives: 122 us -> 0 us
  Pallas kernels: 0 us -> 117 us
  matrix products: 108 us -> 0 us
  other arithmetic: 61 us -> 8.09 us
  local copies, waits for them, and re-layouts: 37.2 us -> 23.7 us
  between operations: 20.6 us -> 9.18 us
    psum x3 -> x0, waiting for transfers between devices: 318 us -> none  [the longest x2 213 us: per_device(): lax.psum((block_total * factor, block_out * factor[..., None]), 'ctx')]
    pmax x1 -> x0, blocking collectives: 122 us -> none  [per_device(): lax.pmax(block_max.astype(jnp.bfloat16), 'ctx').astype(block_max.dtype)]
    pallas_call x0 -> x1, Pallas kernels: none -> 117 us  [per_device(): pl.pallas_call(kernel, out_shape=jax.ShapeDtypeStruct((NC * R // 4, width...]
    dot_general x5 -> x0, matrix products: 108 us -> none  [the longest x2 56.7 us: per_device(): jnp.einsum('qkgs,skd->qkgd', weights.astype(jnp.bfloat16), value_heads, p...]
    reduce_sum x1, other arithmetic: 42.6 us -> 1.41 us  [per_device(): begin = jnp.where(doc == d, jnp.sum((early < d).astype(jnp.int32)), begin)]
    reduce_scatter x1 -> x0, waiting for transfers between devices: 22 us -> none  [per_device(): lax.psum_scatter(jnp.dot(attention, out_weight, preferred_element_type=jn...]
    reshape x6 -> x1, local copies, waits for them, and re-layouts: 21.3 us -> 6.39 us  [per_device(): jnp.concatenate(own, 0).reshape(NC * R, 2 * G, DH).transpose(1, 0, 2)]
    mul x4 -> x0, other arithmetic: 8.96 us -> none  [the longest x2 7.71 us: per_device(): block_out * factor[..., None]]
  transfers between devices with their start and end apart: 4 -> 0, of which waited for: 4 -> 0; matrix products, arithmetic and copies ran while one was open for 2% -> 0% of each run, Pallas kernels for 0% -> 0%
where the time goes in v1:
time: 159 us; the launch traced here: 158 us
  Pallas kernels  117 us (74%)
  local copies, waits for them, and re-layouts  23.7 us (15%)
  between operations  9.18 us (6%)
  other arithmetic  8.09 us (5%)
    pallas_call x1, Pallas kernels, per_device(): pl.pallas_call(kernel, out_shape=jax.ShapeDtypeStruct((NC * R // 4, width...  117 us
    unnamed x7, local copies, waits for them, and re-layouts  8.37 us
    reshape x1, local copies, waits for them, and re-layouts, per_device(): jnp.concatenate(own, 0).reshape(NC * R, 2 * G, DH).transpose(1, 0, 2)  6.39 us
    dynamic_slice x1, local copies, waits for them, and re-layouts, per_device(): block = lax.dynamic_slice_in_dim(queries, query_offset[which], QC, 0)  5.56 us

profile of v1, /device:TPU:1, one launch (start us, length us, event | category | flops | bytes accessed | tf_op | source)
XLA Modules:
  0.0 158.3 jit_solution(6320811292438242131)
XLA Ops:
  0.0 1.3 fusion.5
  5.2 5.6 %constant_dynamic-slice_fusion.1 = (bf16[512,2048]{1,0:T(8,128)(2,1)}, bf16[512,2048]{1,0:T(8,128)(2,1)}) fusion(bf16[2048,2048]{1,0:T(8,128)(2,1)} %param.7, s32[]{:T(128)S(6)} %select_n.40, s32[]{:T(128)S(6)} %select_n.43), kind=kLoop, calls=%fused_computation.17 | loop fusion | bytes 8388616 | tf_op jit(solution)/shard_map/dynamic_slice | solution.py:295
  10.7 2.9 %copy.11 = bf16[512,2048]{0,1:T(8,128)(2,1)S(1)} copy(bf16[512,2048]{1,0:T(8,128)(2,1)} %get-tuple-element.8) | data formatting | bytes 4194304
  13.6 0.0 copy-start.1
  13.6 3.9 %copy.12 = bf16[512,2048]{0,1:T(8,128)(2,1)} copy(bf16[512,2048]{1,0:T(8,128)(2,1)} %get-tuple-element.9) | data formatting | bytes 4194304
  17.6 0.0 copy-done.1
  17.6 0.6 fusion.4
  19.4 0.3 broadcast_select_fusion
  19.7 2.6 %pad_maximum_fusion = bf16[1024,2048]{0,1:T(8,128)(2,1)} fusion(bf16[512,2048]{0,1:T(8,128)(2,1)S(1)} %get-tuple-element.18, bf16[512,2048]{0,1:T(8,128)(2,1)S(1)} %get-tuple-element.19), kind=kLoop, calls=%fused_computation | loop fusion | flops 8388608 | bytes 8388608 | tf_op jit(solution)/shard_map/concatenate | solution.py:299
  22.3 0.0 copy-start
  22.3 6.4 %copy.10 = bf16[1024,16,128]{2,0,1:T(8,128)(2,1)} copy(bf16[1024,16,128]{0,2,1:T(8,128)(2,1)} %bitcast.13) | data formatting | bytes 8388608 | tf_op jit(solution)/shard_map/reshape | solution.py:299
  28.7 0.0 copy-done
  28.7 0.7 fusion.3
  33.4 0.8 dynamic-slice_bitcast_fusion.1
  34.2 0.7 fusion.1
  34.9 0.7 fusion.2
  35.6 1.4 convert_reduce_fusion.2
  37.0 2.4 %fusion = (f32[8,128]{1,0:T(8,128)}, f32[8,128]{1,0:T(8,128)}) fusion(s32[4,128]{1,0:T(4,128)S(1)} %fusion.1, s32[4,128]{1,0:T(4,128)S(1)} %fusion.2, s32[]{:T(128)S(6)} %mul.8, s32[]{:T(128)} %get-tuple-element.7, s32[]{:T(128)} %get-tuple-element.6, s32[]{:T(128)} %get-tuple-element.5, s32[4,128]{1,0:T(4,128)S(1)} %get-tuple-element.11, ...), kind=kLoop, calls=%fused_computation.8 | loop fusion | flops 12288 | bytes 16400 | tf_op jit(solution)/shard_map/convert_element_type | solution.py:306
  39.4 117.3 %shard_map.73 = bf16[256,256]{1,0:T(8,128)(2,1)} custom-call(bf16[16,1024,128]{2,1,0:T(8,128)(2,1)} %bitcast.12, bf16[2048,256]{1,0:T(8,128)(2,1)} %k_ref.1, bf16[2048,256]{1,0:T(8,128)(2,1)} %v_ref.1, bf16[2048,256]{1,0:T(8,128)(2,1)} %w_ref.1, f32[8,128]{1,0:T(8,128)} %get-tuple-element.21.lo_ref, f32[8,128]{1,0:T(8,128)} %get-tuple-element.20.hi_ref), custom_call_target="tpu_custom_call" | custom-call | tf_op jit(solution)/shard_map/pallas_call | solution.py:338
  156.7 1.6 copy.14
  (1 shorter events, 0.0 us)
Async XLA Ops:
  13.6 3.9 %copy-start.1 = (s32[2]{0:T(128)S(1)}, s32[2]{0:T(128)}, u32[]{:S(2)}) copy-start(s32[2]{0:T(128)} %param.11) | copy-start | bytes 28
  22.3 6.4 %copy-start = (s32[2]{0:T(128)S(1)}, s32[2]{0:T(128)}, u32[]{:S(2)}) copy-start(s32[2]{0:T(128)} %param.12) | copy-start | bytes 28

commit v2 on v1

--- a/solution.py
+++ b/solution.py
@@ -25,13 +25,22 @@
 
 
 def kernel(
-    q_own, k_ref, v_ref, w_ref, lo_ref, hi_ref, out_ref,
+    queries, keys, values, weight, early_ref, owner_ref, offset_ref, out_ref,
+    q_all, k_ref, v_ref, w_ref, load, q_send, q_mine,
     kx, vx, qx, s_buf, p_buf,
     u_buf, r1, t_buf, r2, q_full,
     o_send, o_recv, o_own, o_mix, o_two, w_col, o1_send, r1o, o2_send, r2o, a_full,
     y_send, y_recv, send, recv,
 ):
     shard = k_ref.shape[0]
+    loads = [
+        pltpu.make_async_copy(queries, q_all, load.at[0]),
+        pltpu.make_async_copy(keys, k_ref, load.at[1]),
+        pltpu.make_async_copy(values, v_ref, load.at[2]),
+        pltpu.make_async_copy(weight, w_ref, load.at[3]),
+    ]
+    for one in loads:
+        one.start()
     me = lax.axis_index("ctx")
     hd = lax.axis_index("head")
     core = lax.rem(me, 2)
@@ -57,13 +66,18 @@
     pl.semaphore_signal(barrier, inc=1, device_id=partner, device_id_type=MESH)
 
     eye = lax.broadcasted_iota(jnp.int32, (R, R), 0) == lax.broadcasted_iota(jnp.int32, (R, R), 1)
-    for j in range(2):
-        kx[j, 0:DH, :] = k_ref[:, j * DH : (j + 1) * DH].T
-        vx[j, :, 0:DH] = v_ref[:, j * DH : (j + 1) * DH]
-        vx[j, :, DH : 2 * DH] = jnp.ones((shard, DH), jnp.bfloat16)
-    for g in range(G):
-        qx[g * R : (g + 1) * R, DH : 2 * DH] = jnp.where(eye, 1.0, 0.0).astype(jnp.bfloat16)
-
+
+    def prepare():
+        for one in loads[1:]:
+            one.wait()
+        for j in range(2):
+            kx[j, 0:DH, :] = k_ref[:, j * DH : (j + 1) * DH].T
+            vx[j, :, 0:DH] = v_ref[:, j * DH : (j + 1) * DH]
+            vx[j, :, DH : 2 * DH] = jnp.ones((shard, DH), jnp.bfloat16)
+        for g in range(G):
+            qx[g * R : (g + 1) * R, DH : 2 * DH] = jnp.where(eye, 1.0, 0.0).astype(jnp.bfloat16)
+
+    loads[0].wait()
     pl.semaphore_wait(barrier, 10)
 
     def put(src, dst, step, c, dev):
@@ -76,19 +90,26 @@
         pltpu.make_async_copy(like, like, send.at[step, c]).wait()
         pltpu.make_async_copy(like, like, recv.at[step, c]).wait()
 
-    def rows(c):
-        return pl.ds(pl.multiple_of(c * R, R), R)
-
     def quarter(i):
         return pl.ds(pl.multiple_of(i * 32, 32), 32)
 
     def q0_start(c):
-        put(q_own.at[pl.ds(theirs, G), rows(c)], u_buf.at[c], S0, c, partner)
+        which = c // (NC // NCH)
+        row = lax.broadcasted_iota(jnp.int32, (R, shard), 0) + (offset_ref[which] + lax.rem(c, NC // NCH) * R)
+        here = (jnp.zeros((R, shard), jnp.int32) + owner_ref[which]) == me
+        hit = (row == lax.broadcasted_iota(jnp.int32, (R, shard), 1)) & here
+        pick = jnp.where(hit, 1.0, 0.0).astype(jnp.bfloat16)
+        got = jnp.dot(pick, q_all[...], preferred_element_type=jnp.float32).astype(jnp.bfloat16)
+        for g in range(G):
+            low, high = got[:, g * DH : (g + 1) * DH], got[:, (G + g) * DH : (G + g + 1) * DH]
+            q_mine[g] = jnp.where(core == 0, low, high)
+            q_send[g] = jnp.where(core == 0, high, low)
+        put(q_send, u_buf.at[c], S0, c, partner)
 
     def q1_start(c):
         get(u_buf.at[c], S0, c)
         for g in range(G):
-            u_buf[c, g] = u_buf[c, g] + q_own[mine + g, rows(c), :]
+            u_buf[c, g] = u_buf[c, g] + q_mine[g]
         for d in (1, 2, 3):
             put(u_buf.at[c, lax.rem(x + d, 4)], r1.at[c, d - 1], S1, c, at_x(d))
             put(u_buf.at[c, 4 + lax.rem(z + d, 4)], r1.at[c, 2 + d], S1, c, at_z(d))
@@ -127,8 +148,17 @@
         gather1(q_full, c, G1)
 
     def hide(c):
-        lo = jnp.broadcast_to(lo_ref[pl.ds(c, 1), :], (R, R)).T
-        hi = jnp.broadcast_to(hi_ref[pl.ds(c, 1), :], (R, R)).T
+        which = c // (NC // NCH)
+        begin = owner_ref[which] * shard + offset_ref[which] + lax.rem(c, NC // NCH) * R
+        pos = (lax.broadcasted_iota(jnp.int32, (R, R), 0) + begin).astype(jnp.float32)
+        lo = jnp.zeros((R, R), jnp.float32)
+        early = early_ref[...]
+        for d in range(1, 4):
+            bound = jnp.sum(jnp.where(early < d, 1.0, 0.0), axis=0, keepdims=True)
+            bound = jnp.broadcast_to(jnp.sum(bound, axis=1, keepdims=True), (R, R))
+            lo = jnp.where((bound <= pos) & (bound < float(shard)), jnp.maximum(lo, bound), lo)
+        here = (jnp.zeros((R, R), jnp.int32) + me * shard).astype(jnp.float32)
+        lo, hi = lo - here, pos - here
         lane = lax.broadcasted_iota(jnp.int32, (R, R), 1).astype(jnp.float32)
         for i in range(shard // R):
             pos = lane + float(i * R)
@@ -247,20 +277,20 @@
         def when(c, do):
             pl.when((c >= 0) & (c < NC))(functools.partial(do, c))
 
-        when(t, lambda c: get(u_buf.at[c], G3, c))
+        def first(c):
+            get(u_buf.at[c], G3, c)
+            hide(c)
+            attend(c, 1 - core, o_send)
+            put(o_send, o_recv.at[c], O0, c, partner)
+
+        when(t, first)
         when(t + 1, lambda c: gather3(q_full, c, G3))
         when(t + 2, lambda c: gather2(q_full, c, G2))
         when(t + 3, q3_start)
         when(t + 4, q2_start)
         when(t + 5, q1_start)
         when(t + 6, q0_start)
-
-        def first(c):
-            hide(c)
-            attend(c, 1 - core, o_send)
-            put(o_send, o_recv.at[c], O0, c, partner)
-
-        when(t, first)
+        pl.when(t == 1 - LEAD)(prepare)
         when(t, lambda c: attend(c, core, o_own))
         when(t - 5, project)
         when(t - 4, lambda c: gather3(a_full, c, H3))
@@ -287,27 +317,18 @@
 
 
 def per_device(queries, keys_cache, values_cache, doc_ids, query_owner, query_offset, out_weight):
-    me = lax.axis_index("ctx")
     shard = keys_cache.shape[0]
-    starts = query_owner * shard + query_offset
-    own, positions, docs = [], [], []
-    for which in range(NCH):
-        block = lax.dynamic_slice_in_dim(queries, query_offset[which], QC, 0)
-        own.append(jnp.where(query_owner[which] == me, block, jnp.zeros_like(block)))
-        positions.append(starts[which] + jnp.arange(QC, dtype=jnp.int32))
-        docs.append(lax.dynamic_slice_in_dim(doc_ids, starts[which], QC, 0))
-    q_own = jnp.concatenate(own, 0).reshape(NC * R, 2 * G, DH).transpose(1, 0, 2)
-    position, doc = jnp.concatenate(positions), jnp.concatenate(docs)
-    early = doc_ids[:shard]
-    begin = jnp.zeros_like(position)
-    for d in range(1, 4):
-        begin = jnp.where(doc == d, jnp.sum((early < d).astype(jnp.int32)), begin)
-    lo = (begin - me * shard).astype(jnp.float32).reshape(NC, R)
-    hi = (position - me * shard).astype(jnp.float32).reshape(NC, R)
-
+    early = doc_ids[:shard].reshape(-1, DH)
     width = out_weight.shape[1]
     bf, f32 = jnp.bfloat16, jnp.float32
     scratch = [
+        pltpu.VMEM(queries.shape, bf),
+        pltpu.VMEM(keys_cache.shape, bf),
+        pltpu.VMEM(values_cache.shape, bf),
+        pltpu.VMEM(out_weight.shape, bf),
+        pltpu.SemaphoreType.DMA((4,)),
+        pltpu.VMEM((G, R, DH), bf),
+        pltpu.VMEM((G, R, DH), bf),
         pltpu.VMEM((2, 2 * DH, shard), bf),
         pltpu.VMEM((2, shard, 2 * DH), bf),
         pltpu.VMEM((G * R, 2 * DH), bf),
@@ -338,13 +359,14 @@
     return pl.pallas_call(
         kernel,
         out_shape=jax.ShapeDtypeStruct((NC * R // 4, width), bf),
-        in_specs=[vmem] * 6,
+        in_specs=[pl.BlockSpec(memory_space=pl.ANY)] * 4
+        + [vmem] + [pl.BlockSpec(memory_space=pltpu.SMEM)] * 2,
         out_specs=vmem,
         scratch_shapes=scratch,
         compiler_params=pltpu.CompilerParams(
             collective_id=0, has_side_effects=True, vmem_limit_bytes=60 * 2**20
         ),
-    )(q_own, keys_cache, values_cache, out_weight, lo, hi)
+    )(queries, keys_cache, values_cache, out_weight, early, query_owner, query_offset)
 
 
 def solution(mesh):

time: 159 us -> 124 us (0.78)
  local copies, waits for them, and re-layouts: 23.7 us -> 2.86 us
  between operations: 9.18 us -> 0.01 us
  other arithmetic: 8.09 us -> 0 us
  Pallas kernels: 117 us -> 121 us
    unnamed x7 -> x1, local copies, waits for them, and re-layouts: 8.37 us -> 1.57 us
    reshape x1 -> x0, local copies, waits for them, and re-layouts: 6.39 us -> none  [per_device(): jnp.concatenate(own, 0).reshape(NC * R, 2 * G, DH).transpose(1, 0, 2)]
    dynamic_slice x1 -> x0, local copies, waits for them, and re-layouts: 5.56 us -> none  [per_device(): block = lax.dynamic_slice_in_dim(queries, query_offset[which], QC, 0)]
    pallas_call x1, Pallas kernels: 117 us -> 121 us  [per_device(): pl.pallas_call(kernel, out_shape=jax.ShapeDtypeStruct((NC * R // 4, width...]
    concatenate x1 -> x0, other arithmetic: 2.62 us -> none  [per_device(): jnp.concatenate(own, 0).reshape(NC * R, 2 * G, DH).transpose(1, 0, 2)]
    convert_element_type x1 -> x0, other arithmetic: 2.42 us -> none  [per_device(): hi = (position - me * shard).astype(jnp.float32).reshape(NC, R)]
where the time goes in v2:
time: 124 us
  Pallas kernels  121 us (98%)
  local copies, waits for them, and re-layouts  2.86 us (2%)
    pallas_call x1, Pallas kernels, per_device(): pl.pallas_call(kernel, out_shape=jax.ShapeDtypeStruct((NC * R // 4, width...  121 us

profile of v2, /device:TPU:1, one launch (start us, length us, event | category | flops | bytes accessed | tf_op | source)
XLA Modules:
  0.0 123.6 jit_solution(8843009204227182540)
XLA Ops:
  0.0 1.3 %slice_bitcast_fusion.early_ref = s32[16,128]{1,0:T(8,128)} fusion(s32[65536]{0:T(1024)} %param.10), kind=kLoop, calls=%fused_computation | loop fusion | bytes 16384 | tf_op jit(solution)/shard_map/slice | solution.py:321
  1.3 120.8 %shard_map.73 = bf16[256,256]{1,0:T(8,128)(2,1)} custom-call(bf16[2048,2048]{1,0:T(8,128)(2,1)} %queries.1, bf16[2048,256]{1,0:T(8,128)(2,1)} %keys.1, bf16[2048,256]{1,0:T(8,128)(2,1)} %values.1, bf16[2048,256]{1,0:T(8,128)(2,1)} %weight.1, s32[16,128]{1,0:T(8,128)} %slice_bitcast_fusion.early_ref, s32[2]{0:T(128)} %owner_ref.1, s32[2]{0:T(128)} %offset_ref.1), custom_call_target="tpu_custom_call" | custom-call | tf_op jit(solution)/shard_map/pallas_call | solution.py:359
  122.1 1.6 %copy.9 = bf16[256,256]{1,0:T(8,128)(2,1)} copy(bf16[256,256]{1,0:T(8,128)(2,1)} %shard_map.73) | data formatting | bytes 262144

commit v3 on v2

--- a/solution.py
+++ b/solution.py
@@ -18,18 +18,18 @@
 HIDE = -1e30
 SCALE = math.log2(math.e) / math.sqrt(DH)
 MESH = pl.DeviceIdType.MESH
-LEAD = 6
-TRAIL = 6
+LEAD = 5
+TRAIL = 5
 
 S0, S1, S2, G1, G2, G3, O0, O1, O2, H1, H2, H3, Y = range(13)
 
 
 def kernel(
-    queries, keys, values, weight, early_ref, owner_ref, offset_ref, out_ref,
-    q_all, k_ref, v_ref, w_ref, load, q_send, q_mine,
+    queries, keys, values, weight, docs, owner_ref, offset_ref, out_ref,
+    q_all, k_ref, v_ref, w_ref, early_ref, load, q_send, q_mine,
     kx, vx, qx, s_buf, p_buf,
-    u_buf, r1, t_buf, r2, q_full,
-    o_send, o_recv, o_own, o_mix, o_two, w_col, o1_send, r1o, o2_send, r2o, a_full,
+    u_buf, r1, t_buf, r2, x2, q_full,
+    o_send, o_recv, o_own, o_mix, o_two, o1_send, r1o, o2_send, r2o, x2_send, x2o, w_col, a_full, a_cat,
     y_send, y_recv, send, recv,
 ):
     shard = k_ref.shape[0]
@@ -38,6 +38,7 @@
         pltpu.make_async_copy(keys, k_ref, load.at[1]),
         pltpu.make_async_copy(values, v_ref, load.at[2]),
         pltpu.make_async_copy(weight, w_ref, load.at[3]),
+        pltpu.make_async_copy(docs.at[pl.ds(0, shard // DH)], early_ref, load.at[4]),
     ]
     for one in loads:
         one.start()
@@ -77,8 +78,6 @@
         for g in range(G):
             qx[g * R : (g + 1) * R, DH : 2 * DH] = jnp.where(eye, 1.0, 0.0).astype(jnp.bfloat16)
 
-    loads[0].wait()
-    pl.semaphore_wait(barrier, 10)
 
     def put(src, dst, step, c, dev):
         pltpu.make_async_remote_copy(
@@ -93,7 +92,7 @@
     def quarter(i):
         return pl.ds(pl.multiple_of(i * 32, 32), 32)
 
-    def q0_start(c):
+    def pick_rows(c):
         which = c // (NC // NCH)
         row = lax.broadcasted_iota(jnp.int32, (R, shard), 0) + (offset_ref[which] + lax.rem(c, NC // NCH) * R)
         here = (jnp.zeros((R, shard), jnp.int32) + owner_ref[which]) == me
@@ -102,25 +101,37 @@
         got = jnp.dot(pick, q_all[...], preferred_element_type=jnp.float32).astype(jnp.bfloat16)
         for g in range(G):
             low, high = got[:, g * DH : (g + 1) * DH], got[:, (G + g) * DH : (G + g + 1) * DH]
-            q_mine[g] = jnp.where(core == 0, low, high)
-            q_send[g] = jnp.where(core == 0, high, low)
-        put(q_send, u_buf.at[c], S0, c, partner)
+            q_mine[lax.rem(c, 2), g] = jnp.where(core == 0, low, high)
+            q_send[lax.rem(c, 2), g] = jnp.where(core == 0, high, low)
+
+    def q0_start(c):
+        pick_rows(c)
+        put(q_send.at[lax.rem(c, 2)], u_buf.at[c], S0, c, partner)
 
     def q1_start(c):
         get(u_buf.at[c], S0, c)
         for g in range(G):
-            u_buf[c, g] = u_buf[c, g] + q_mine[g]
+            u_buf[c, g] = u_buf[c, g] + q_mine[lax.rem(c, 2), g]
         for d in (1, 2, 3):
             put(u_buf.at[c, lax.rem(x + d, 4)], r1.at[c, d - 1], S1, c, at_x(d))
             put(u_buf.at[c, 4 + lax.rem(z + d, 4)], r1.at[c, 2 + d], S1, c, at_z(d))
 
-    def q2_start(c):
+    def sum1(c):
         get(r1.at[c], S1, c)
         t_buf[c, 0] = (u_buf[c, x] + r1[c, 0]) + (r1[c, 1] + r1[c, 2])
         t_buf[c, 1] = (u_buf[c, 4 + z] + r1[c, 3]) + (r1[c, 4] + r1[c, 5])
+
+    def q2_start(c):
+        sum1(c)
         for d in (1, 2, 3):
             put(t_buf.at[c, 0, quarter(lax.rem(z + d, 4))], r2.at[c, d - 1], S2, c, at_z(d))
             put(t_buf.at[c, 1, quarter(lax.rem(x + d, 4))], r2.at[c, 2 + d], S2, c, at_x(d))
+
+    def q2_first(c):
+        sum1(c)
+        for d in (1, 2, 3):
+            put(t_buf.at[c, 0], x2.at[d - 1], S2, c, at_z(d))
+            put(t_buf.at[c, 1], x2.at[2 + d], S2, c, at_x(d))
 
     def gather1(full, c, step):
         a = full.at[c, mine + x, quarter(z)]
@@ -130,7 +141,6 @@
             put(b, b, step, c, at_x(d))
 
     def gather2(full, c, step):
-        get(r2.at[c], step - 1, c)
         a, b = full.at[c, mine + x], full.at[c, mine + 4 + z]
         for d in (1, 2, 3):
             put(a, a, step, c, at_x(d))
@@ -146,6 +156,16 @@
         q_full[c, mine + x, quarter(z), :] = (t_buf[c, 0, quarter(z), :] + r2[c, 0]) + (r2[c, 1] + r2[c, 2])
         q_full[c, mine + 4 + z, quarter(x), :] = (t_buf[c, 1, quarter(x), :] + r2[c, 3]) + (r2[c, 4] + r2[c, 5])
         gather1(q_full, c, G1)
+
+    def q3_first(c):
+        get(x2, S2, c)
+        q_full[c, mine + x] = (t_buf[c, 0] + x2[0]) + (x2[1] + x2[2])
+        q_full[c, mine + 4 + z] = (t_buf[c, 1] + x2[3]) + (x2[4] + x2[5])
+        gather2(q_full, c, G2)
+
+    def q4_start(c):
+        get(r2.at[c], G1, c)
+        gather2(q_full, c, G2)
 
     def hide(c):
         which = c // (NC // NCH)
@@ -214,57 +234,79 @@
         f = block.astype(jnp.float32)
         return (f[0:1] + f[1:2]) + f[2:3]
 
-    def o1_start(c):
-        get(o_recv.at[c], O0, c)
+    def merge1(c, side):
         for g in range(G):
-            (wa, wb), lse = merge_stats([o_own[g, R : R + 1, :], o_recv[c, g, R : R + 1, :]])
-            mixed = o_own[g, 0:R, :] * column(wa) + o_recv[c, g, 0:R, :] * column(wb)
-            o_mix[g, 0:R, :] = mixed
-            o_mix[g, R : R + 8, :] = jnp.broadcast_to(lse, (8, R))
-            o1_send[c, g, 0:R, :] = mixed.astype(jnp.bfloat16)
-            o1_send[c, g, R : R + 16, :] = pieces3(lse)
-        for d in (1, 2, 3):
-            put(o1_send.at[c, lax.rem(x + d, 4)], r1o.at[c, d - 1], O1, c, at_x(d))
-            put(o1_send.at[c, 4 + lax.rem(z + d, 4)], r1o.at[c, 2 + d], O1, c, at_z(d))
-
-    def o2_start(c):
-        get(r1o.at[c], O1, c)
+            (wa, _), lse = merge_stats([o_own[g, R : R + 1, :], o_recv[c, g, R : R + 1, :]])
+            wa = column(wa)
+            mixed = o_own[g, 0:R, :] * wa + o_recv[c, g, 0:R, :] * (1.0 - wa)
+            o_mix[side, g, 0:R, :] = mixed
+            o_mix[side, g, R : R + 8, :] = jnp.broadcast_to(lse, (8, R))
+            o1_send[side, g, 0:R, :] = mixed.astype(jnp.bfloat16)
+            o1_send[side, g, R : R + 16, :] = pieces3(lse)
+
+    def send1(c):
+        for d in (1, 2, 3):
+            put(o1_send.at[lax.rem(c, 2), lax.rem(x + d, 4)], r1o.at[c, d - 1], O1, c, at_x(d))
+            put(o1_send.at[lax.rem(c, 2), 4 + lax.rem(z + d, 4)], r1o.at[c, 2 + d], O1, c, at_z(d))
+
+    def merge_four(own, others):
+        stats = [own[R : R + 1, :]] + [whole3(o[R : R + 16, :]) for o in others]
+        ws, lse = merge_stats(stats)
+        mixed = own[0:R, :] * column(ws[0])
+        for o, w in zip(others, ws[1:]):
+            mixed += o[0:R, :].astype(jnp.float32) * column(w)
+        return mixed, lse
+
+    def merge2(c, side):
         for i, at in ((0, x), (1, 4 + z)):
-            stats = [o_mix[at, R : R + 1, :]] + [whole3(r1o[c, 3 * i + d, R : R + 16, :]) for d in range(3)]
-            ws, lse = merge_stats(stats)
-            mixed = o_mix[at, 0:R, :] * column(ws[0])
-            for d in range(3):
-                mixed += r1o[c, 3 * i + d, 0:R, :].astype(jnp.float32) * column(ws[1 + d])
-            o_two[i, 0:R, :] = mixed
-            o_two[i, R : R + 8, :] = jnp.broadcast_to(lse, (8, R))
+            mixed, lse = merge_four(o_mix[side, at], [r1o[c, 3 * i + d] for d in range(3)])
+            o_two[side, i, 0:R, :] = mixed
+            o_two[side, i, R : R + 8, :] = jnp.broadcast_to(lse, (8, R))
             coded = pieces3(lse)
             for q in range(4):
-                o2_send[c, i, q, 0:32, :] = mixed[q * 32 : (q + 1) * 32].astype(jnp.bfloat16)
-                o2_send[c, i, q, 32:48, :] = coded
+                o2_send[side, i, q, 0:32, :] = mixed[q * 32 : (q + 1) * 32].astype(jnp.bfloat16)
+                o2_send[side, i, q, 32:48, :] = coded
+
+    def send2(c):
         for d in (1, 2, 3):
             zd, xd = lax.rem(z + d, 4), lax.rem(x + d, 4)
-            put(o2_send.at[c, 0, zd], r2o.at[c, d - 1], O2, c, at_z(d))
-            put(o2_send.at[c, 1, xd], r2o.at[c, 2 + d], O2, c, at_x(d))
-
-    def o3_start(c):
-        get(r2o.at[c], O2, c)
+            put(o2_send.at[lax.rem(c, 2), 0, zd], r2o.at[c, d - 1], O2, c, at_z(d))
+            put(o2_send.at[lax.rem(c, 2), 1, xd], r2o.at[c, 2 + d], O2, c, at_x(d))
+
+    def merge3(c, side):
         for i, at, part in ((0, x, z), (1, 4 + z, x)):
-            stats = [o_two[i, R : R + 1, :]] + [whole3(r2o[c, 3 * i + d, 32:48, :]) for d in range(3)]
+            stats = [o_two[side, i, R : R + 1, :]] + [whole3(r2o[c, 3 * i + d, 32:48, :]) for d in range(3)]
             ws, _ = merge_stats(stats)
             for d in range(4):
-                w_col[d] = column(ws[d])
-            mixed = o_two[i, quarter(part), :] * w_col[0, quarter(part), :]
+                w_col[i, d] = column(ws[d])
+            mixed = o_two[side, i, quarter(part), :] * w_col[i, 0, quarter(part), :]
             for d in range(3):
-                mixed += r2o[c, 3 * i + d, 0:32, :].astype(jnp.float32) * w_col[1 + d, quarter(part), :]
+                mixed += r2o[c, 3 * i + d, 0:32, :].astype(jnp.float32) * w_col[i, 1 + d, quarter(part), :]
             a_full[c, mine + at, quarter(part), :] = mixed.astype(jnp.bfloat16)
-        gather1(a_full, c, H1)
+
+    def merge2_last(c, side):
+        for i, at in ((0, x), (1, 4 + z)):
+            mixed, lse = merge_four(o_mix[side, at], [r1o[c, 3 * i + d] for d in range(3)])
+            o_two[side, i, 0:R, :] = mixed
+            o_two[side, i, R : R + 8, :] = jnp.broadcast_to(lse, (8, R))
+            x2_send[i, 0:R, :] = mixed.astype(jnp.bfloat16)
+            x2_send[i, R : R + 16, :] = pieces3(lse)
+        for d in (1, 2, 3):
+            put(x2_send.at[0], x2o.at[d - 1], O2, c, at_z(d))
+            put(x2_send.at[1], x2o.at[2 + d], O2, c, at_x(d))
+
+    def merge3_last(c, side):
+        get(x2o, O2, c)
+        for i, at in ((0, x), (1, 4 + z)):
+            mixed, _ = merge_four(o_two[side, i], [x2o[3 * i + d] for d in range(3)])
+            a_full[c, mine + at] = mixed.astype(jnp.bfloat16)
+        gather2(a_full, c, H2)
 
     def project(c):
         get(a_full.at[c, pl.ds(0, G)], H3, c)
-        acc = jnp.zeros((R, w_ref.shape[1]), jnp.float32)
         for h in range(2 * G):
-            acc += jnp.dot(a_full[c, h], w_ref[h * DH : (h + 1) * DH, :], preferred_element_type=jnp.float32)
-        y_send[c] = acc
+            a_cat[:, h * DH : (h + 1) * DH] = a_full[c, h]
+        y_send[c] = jnp.dot(a_cat[...], w_ref[...], preferred_element_type=jnp.float32)
         owner = c // 2
         slot = lax.rem(c, 2)
         d = lax.rem(owner - hd + 4, 4)
@@ -273,34 +315,118 @@
         def _():
             put(y_send.at[c], y_recv.at[d - 1, slot], Y, c, at_y(d))
 
-    def slot(t, carry):
-        def when(c, do):
-            pl.when((c >= 0) & (c < NC))(functools.partial(do, c))
-
-        def first(c):
-            get(u_buf.at[c], G3, c)
-            hide(c)
-            attend(c, 1 - core, o_send)
-            put(o_send, o_recv.at[c], O0, c, partner)
-
-        when(t, first)
+    def when(c, do):
+        pl.when((c >= 0) & (c < NC))(functools.partial(do, c))
+
+    def when_in(c, first, last, do):
+        pl.when((c >= first) & (c <= last))(functools.partial(do, c))
+
+    def query_steps(t):
+        def only(at, do):
+            pl.when(t == at)(functools.partial(do, 0))
+
+        only(-2, q3_first)
+        only(-3, q2_first)
+        only(-4, q1_start)
         when(t + 1, lambda c: gather3(q_full, c, G3))
-        when(t + 2, lambda c: gather2(q_full, c, G2))
-        when(t + 3, q3_start)
-        when(t + 4, q2_start)
-        when(t + 5, q1_start)
-        when(t + 6, q0_start)
+        when_in(t + 2, 1, NC - 1, q4_start)
+        when_in(t + 3, 1, NC - 1, q3_start)
+        when_in(t + 4, 1, NC - 1, q2_start)
+        when_in(t + 5, 1, NC - 1, q1_start)
+        when_in(t + 6, 1, NC - 1, q0_start)
+
+    def before(t, carry):
+        query_steps(t)
         pl.when(t == 1 - LEAD)(prepare)
-        when(t, lambda c: attend(c, core, o_own))
-        when(t - 5, project)
-        when(t - 4, lambda c: gather3(a_full, c, H3))
-        when(t - 3, lambda c: gather2(a_full, c, H2))
-        when(t - 2, o3_start)
-        when(t - 1, o2_start)
-        when(t, o1_start)
         return carry
 
-    lax.fori_loop(-LEAD, NC + TRAIL - 1, slot, 0)
+    def valid(c):
+        return jnp.where(c < 0, NC, c)
+
+    o_own[...] = jnp.zeros_like(o_own)
+    o_mix[...] = jnp.zeros_like(o_mix)
+    o_two[...] = jnp.zeros_like(o_two)
+    o_recv[NC] = jnp.zeros(o_recv.shape[1:], jnp.float32)
+    r1o[NC] = jnp.zeros(r1o.shape[1:], jnp.bfloat16)
+    r2o[NC] = jnp.zeros(r2o.shape[1:], jnp.bfloat16)
+
+    def h2_start(c):
+        get(r2.at[c], H1, c)
+        gather2(a_full, c, H2)
+
+    def during(t, carry):
+        even, odd = lax.rem(t, 2), lax.rem(t + 1, 2)
+        get(u_buf.at[t], G3, t)
+        when(t - 1, lambda c: get(o_recv.at[c], O0, c))
+        hide(t)
+        attend(t, 1 - core, o_send)
+        merge1(valid(t - 1), odd)
+        put(o_send, o_recv.at[t], O0, t, partner)
+        when(t - 1, send1)
+        query_steps(t)
+        when(t - 6, project)
+        when(t - 5, lambda c: gather3(a_full, c, H3))
+        when(t - 4, h2_start)
+        when(t - 3, lambda c: get(r2o.at[c], O2, c))
+        when(t - 2, lambda c: get(r1o.at[c], O1, c))
+        attend(t, core, o_own)
+        merge3(valid(t - 3), odd)
+        merge2(valid(t - 2), even)
+        when(t - 2, send2)
+        when(t - 3, lambda c: gather1(a_full, c, H1))
+        return carry
+
+    def after(t, carry):
+        even, odd = lax.rem(t, 2), lax.rem(t + 1, 2)
+
+        def last1(c):
+            get(o_recv.at[c], O0, c)
+            merge1(c, odd)
+            send1(c)
+
+        def last3(c):
+            get(r2o.at[c], O2, c)
+            merge3(c, odd)
+            gather1(a_full, c, H1)
+
+        def last2(c):
+            get(r1o.at[c], O1, c)
+            merge2(c, even)
+            send2(c)
+
+        @pl.when(t == NC + 1)
+        def _():
+            get(r1o.at[NC - 1], O1, NC - 1)
+            merge2_last(NC - 1, (NC - 1) % 2)
+
+        @pl.when(t == NC + 2)
+        def _():
+            merge3_last(NC - 1, (NC - 1) % 2)
+
+        @pl.when(t == NC + 3)
+        def _():
+            gather3(a_full, NC - 1, H3)
+
+        when(t - 1, last1)
+        when_in(t - 3, 0, NC - 2, last3)
+        when_in(t - 2, 0, NC - 2, last2)
+        when_in(t - 4, 0, NC - 2, h2_start)
+        when_in(t - 5, 0, NC - 2, lambda c: gather3(a_full, c, H3))
+        when_in(t - 6, 0, NC - 2, project)
+
+        @pl.when(t == NC + 4)
+        def _():
+            project(NC - 1)
+
+        return carry
+
+    loads[0].wait()
+    pick_rows(0)
+    pl.semaphore_wait(barrier, 10)
+    put(q_send.at[0], u_buf.at[0], S0, 0, partner)
+    lax.fori_loop(-LEAD, 0, before, 0)
+    lax.fori_loop(0, NC, during, 0)
+    lax.fori_loop(NC, NC + TRAIL, after, 0)
 
     for c in range(NC):
         d = lax.rem(c // 2 - hd + 4, 4)
@@ -318,7 +444,7 @@
 
 def per_device(queries, keys_cache, values_cache, doc_ids, query_owner, query_offset, out_weight):
     shard = keys_cache.shape[0]
-    early = doc_ids[:shard].reshape(-1, DH)
+    docs = doc_ids.reshape(-1, DH)
     width = out_weight.shape[1]
     bf, f32 = jnp.bfloat16, jnp.float32
     scratch = [
@@ -326,9 +452,10 @@
         pltpu.VMEM(keys_cache.shape, bf),
         pltpu.VMEM(values_cache.shape, bf),
         pltpu.VMEM(out_weight.shape, bf),
-        pltpu.SemaphoreType.DMA((4,)),
-        pltpu.VMEM((G, R, DH), bf),
-        pltpu.VMEM((G, R, DH), bf),
+        pltpu.VMEM((shard // DH, DH), jnp.int32),
+        pltpu.SemaphoreType.DMA((5,)),
+        pltpu.VMEM((2, G, R, DH), bf),
+        pltpu.VMEM((2, G, R, DH), bf),
         pltpu.VMEM((2, 2 * DH, shard), bf),
         pltpu.VMEM((2, shard, 2 * DH), bf),
         pltpu.VMEM((G * R, 2 * DH), bf),
@@ -338,18 +465,22 @@
         pltpu.VMEM((NC, 6, R, DH), bf),
         pltpu.VMEM((NC, 2, R, DH), bf),
         pltpu.VMEM((NC, 6, 32, DH), bf),
+        pltpu.VMEM((6, R, DH), bf),
         pltpu.VMEM((NC, 2 * G, R, DH), bf),
         pltpu.VMEM((G, R + 8, DH), f32),
-        pltpu.VMEM((NC, G, R + 8, DH), f32),
+        pltpu.VMEM((NC + 1, G, R + 8, DH), f32),
         pltpu.VMEM((G, R + 8, DH), f32),
-        pltpu.VMEM((G, R + 8, DH), f32),
-        pltpu.VMEM((2, R + 8, DH), f32),
-        pltpu.VMEM((4, R, DH), f32),
-        pltpu.VMEM((NC, G, R + 16, DH), bf),
-        pltpu.VMEM((NC, 6, R + 16, DH), bf),
-        pltpu.VMEM((NC, 2, 4, 48, DH), bf),
-        pltpu.VMEM((NC, 6, 48, DH), bf),
-        pltpu.VMEM((NC, 2 * G, R, DH), bf),
+        pltpu.VMEM((2, G, R + 8, DH), f32),
+        pltpu.VMEM((2, 2, R + 8, DH), f32),
+        pltpu.VMEM((2, G, R + 16, DH), bf),
+        pltpu.VMEM((NC + 1, 6, R + 16, DH), bf),
+        pltpu.VMEM((2, 2, 4, 48, DH), bf),
+        pltpu.VMEM((NC + 1, 6, 48, DH), bf),
+        pltpu.VMEM((2, R + 16, DH), bf),
+        pltpu.VMEM((6, R + 16, DH), bf),
+        pltpu.VMEM((2, 4, R, DH), f32),
+        pltpu.VMEM((NC + 1, 2 * G, R, DH), bf),
+        pltpu.VMEM((R, 2 * G * DH), bf),
         pltpu.VMEM((NC, R, width), f32),
         pltpu.VMEM((3, 2, R, width), f32),
         pltpu.SemaphoreType.DMA((13, NC)),
@@ -359,14 +490,14 @@
     return pl.pallas_call(
         kernel,
         out_shape=jax.ShapeDtypeStruct((NC * R // 4, width), bf),
-        in_specs=[pl.BlockSpec(memory_space=pl.ANY)] * 4
-        + [vmem] + [pl.BlockSpec(memory_space=pltpu.SMEM)] * 2,
+        in_specs=[pl.BlockSpec(memory_space=pl.ANY)] * 5
+        + [pl.BlockSpec(memory_space=pltpu.SMEM)] * 2,
         out_specs=vmem,
         scratch_shapes=scratch,
         compiler_params=pltpu.CompilerParams(
-            collective_id=0, has_side_effects=True, vmem_limit_bytes=60 * 2**20
+            collective_id=0, has_side_effects=True, vmem_limit_bytes=61 * 2**20
         ),
-    )(queries, keys_cache, values_cache, out_weight, early, query_owner, query_offset)
+    )(queries, keys_cache, values_cache, out_weight, docs, query_owner, query_offset)
 
 
 def solution(mesh):

time: 124 us -> 121 us (0.976)
  local copies, waits for them, and re-layouts: 2.86 us -> 1.57 us
    slice x1 -> x0, local copies, waits for them, and re-layouts: 1.29 us -> none  [per_device(): early = doc_ids[:shard].reshape(-1, DH)]
where the time goes in v3:
time: 121 us
  Pallas kernels  120 us (99%)
  local copies, waits for them, and re-layouts  1.57 us (1%)
    pallas_call x1, Pallas kernels, per_device(): pl.pallas_call(kernel, out_shape=jax.ShapeDtypeStruct((NC * R // 4, width...  120 us

profile of v3, /device:TPU:1, one launch (start us, length us, event | category | flops | bytes accessed | tf_op | source)
XLA Modules:
  0.0 121.2 jit_solution(5271680873638772309)
XLA Ops:
  0.0 119.7 %shard_map.73 = bf16[256,256]{1,0:T(8,128)(2,1)} custom-call(bf16[2048,2048]{1,0:T(8,128)(2,1)} %queries.1, bf16[2048,256]{1,0:T(8,128)(2,1)} %keys.1, bf16[2048,256]{1,0:T(8,128)(2,1)} %values.1, bf16[2048,256]{1,0:T(8,128)(2,1)} %weight.1, s32[512,128]{1,0:T(8,128)} %bitcast.1, s32[2]{0:T(128)} %owner_ref.1, s32[2]{0:T(128)} %offset_ref.1), custom_call_target="tpu_custom_call" | custom-call | tf_op jit(solution)/shard_map/pallas_call | solution.py:490
  119.7 1.6 %copy.9 = bf16[256,256]{1,0:T(8,128)(2,1)} copy(bf16[256,256]{1,0:T(8,128)(2,1)} %shard_map.73) | data formatting | bytes 262144

commit v4 on v3

--- a/solution.py
+++ b/solution.py
@@ -86,8 +86,14 @@
         ).start()
 
     def get(like, step, c):
+        pltpu.make_async_copy(like, like, recv.at[step, c]).wait()
+
+    def sent(like, step, c):
         pltpu.make_async_copy(like, like, send.at[step, c]).wait()
-        pltpu.make_async_copy(like, like, recv.at[step, c]).wait()
+
+    def both(like, step, c):
+        sent(like, step, c)
+        get(like, step, c)
 
     def quarter(i):
         return pl.ds(pl.multiple_of(i * 32, 32), 32)
@@ -109,7 +115,7 @@
         put(q_send.at[lax.rem(c, 2)], u_buf.at[c], S0, c, partner)
 
     def q1_start(c):
-        get(u_buf.at[c], S0, c)
+        both(u_buf.at[c], S0, c)
         for g in range(G):
             u_buf[c, g] = u_buf[c, g] + q_mine[lax.rem(c, 2), g]
         for d in (1, 2, 3):
@@ -357,7 +363,7 @@
     def during(t, carry):
         even, odd = lax.rem(t, 2), lax.rem(t + 1, 2)
         get(u_buf.at[t], G3, t)
-        when(t - 1, lambda c: get(o_recv.at[c], O0, c))
+        when(t - 1, lambda c: both(o_recv.at[c], O0, c))
         hide(t)
         attend(t, 1 - core, o_send)
         merge1(valid(t - 1), odd)
@@ -367,8 +373,8 @@
         when(t - 6, project)
         when(t - 5, lambda c: gather3(a_full, c, H3))
         when(t - 4, h2_start)
-        when(t - 3, lambda c: get(r2o.at[c], O2, c))
-        when(t - 2, lambda c: get(r1o.at[c], O1, c))
+        when(t - 3, lambda c: both(r2o.at[c], O2, c))
+        when(t - 2, lambda c: both(r1o.at[c], O1, c))
         attend(t, core, o_own)
         merge3(valid(t - 3), odd)
         merge2(valid(t - 2), even)
@@ -380,17 +386,17 @@
         even, odd = lax.rem(t, 2), lax.rem(t + 1, 2)
 
         def last1(c):
-            get(o_recv.at[c], O0, c)
+            both(o_recv.at[c], O0, c)
             merge1(c, odd)
             send1(c)
 
         def last3(c):
-            get(r2o.at[c], O2, c)
+            both(r2o.at[c], O2, c)
             merge3(c, odd)
             gather1(a_full, c, H1)
 
         def last2(c):
-            get(r1o.at[c], O1, c)
+            both(r1o.at[c], O1, c)
             merge2(c, even)
             send2(c)
 
@@ -427,6 +433,28 @@
     lax.fori_loop(-LEAD, 0, before, 0)
     lax.fori_loop(0, NC, during, 0)
     lax.fori_loop(NC, NC + TRAIL, after, 0)
+
+    def drain(c, carry):
+        for step in (S1, G2, H2):
+            sent(r1.at[c], step, c)
+        for step in (G3, H3):
+            sent(u_buf.at[c], step, c)
+
+        @pl.when(c > 0)
+        def _():
+            sent(r2.at[c], S2, c)
+            sent(r2.at[c], G1, c)
+
+        @pl.when(c < NC - 1)
+        def _():
+            sent(r2.at[c], H1, c)
+
+        return carry
+
+    sent(x2, S2, 0)
+    sent(r1o.at[NC - 1], O1, NC - 1)
+    sent(x2o, O2, NC - 1)
+    lax.fori_loop(0, NC, drain, 0)
 
     for c in range(NC):
         d = lax.rem(c // 2 - hd + 4, 4)

time: 121 us -> 121 us (level)
  no operation moved by 1% of the time
where the time goes in v4:
time: 121 us
  Pallas kernels  119 us (98%)
  local copies, waits for them, and re-layouts  1.57 us (1%)
    pallas_call x1, Pallas kernels, per_device(): pl.pallas_call(kernel, out_shape=jax.ShapeDtypeStruct((NC * R // 4, width...  119 us

profile of v4, /device:TPU:1, one launch (start us, length us, event | category | flops | bytes accessed | tf_op | source)
XLA Modules:
  0.0 121.0 jit_solution(14349810003510848496)
XLA Ops:
  0.0 119.5 %shard_map.73 = bf16[256,256]{1,0:T(8,128)(2,1)} custom-call(bf16[2048,2048]{1,0:T(8,128)(2,1)} %queries.1, bf16[2048,256]{1,0:T(8,128)(2,1)} %keys.1, bf16[2048,256]{1,0:T(8,128)(2,1)} %values.1, bf16[2048,256]{1,0:T(8,128)(2,1)} %weight.1, s32[512,128]{1,0:T(8,128)} %bitcast.1, s32[2]{0:T(128)} %owner_ref.1, s32[2]{0:T(128)} %offset_ref.1), custom_call_target="tpu_custom_call" | custom-call | tf_op jit(solution)/shard_map/pallas_call | solution.py:518
  119.5 1.6 %copy.9 = bf16[256,256]{1,0:T(8,128)(2,1)} copy(bf16[256,256]{1,0:T(8,128)(2,1)} %shard_map.73) | data formatting | bytes 262144
